TPU v7x, 128 devices: a whole 4x4x4 slice. The times are simulated.
128 devices in a mesh: slab: 8 (over z_lo, x), band: 16 (over z_hi, y, core).
Axes of the slice: x: 4, y: 4, z: 4 (z_hi: 2, z_lo: 2; z = z_hi * 2 + z_lo), core: 2. Of those that a mesh axis runs over, the one named last changes fastest.
Arguments:
- orbitals: float32 [384, 96, 2304], P('band', 'slab'), may hold values from -20 to 20
- potential: float32 [96, 2304], P('slab'), may hold values from -3 to 1
Outputs:
- filtered: float32 [384, 96, 2304], P('band', 'slab')
- correlation: float32 [384, 384], P('band', 'slab')
- projected: float32 [384, 384], P('band', 'slab')
All inputs are finite; a program needn't handle non-finite values.
Results may differ from a plain program's by a relative error of at most 0.00016.
Values sent between devices are 32-bit elements; how exact they have to be, the bound alone decides.
A program may use at most 128 MiB of HBM per device.

v0:
```python
import jax
import jax.numpy as jnp
from jax import lax
from jax.sharding import PartitionSpec as P

NX = 48


SPACING = 0.32
STENCIL = 1.0 / (12.0 * SPACING * SPACING)
CENTER = 38.0
HALF_WIDTH = 42.0


def extended_2(block, sides, width):
    for axis, dim in sides:
        count = lax.axis_size(axis)
        forward = [(i, i + 1) for i in range(count - 1)]
        forward.append((count - 1, 0))
        backward = [(target, source) for source, target in forward]
        low = lax.ppermute(
            lax.slice_in_dim(block, block.shape[dim] - width, None, axis=dim), axis, forward
        )
        high = lax.ppermute(lax.slice_in_dim(block, 0, width, axis=dim), axis, backward)
        block = jnp.concatenate([low, block, high], axis=dim)
    return block


def in_plane(grid_field, column_x, width):
    summed = -60.0 * grid_field
    for offset, weight in ((1, 16.0), (2, -1.0), (-1, 16.0), (-2, -1.0)):
        within = (column_x + offset >= 0) & (column_x + offset < width)
        wrap_step = offset - width if offset > 0 else offset + width
        shift_x = jnp.where(
            within,
            jnp.roll(grid_field, -offset, axis=-1),
            jnp.roll(grid_field, -wrap_step, axis=-1),
        )
        shift_y = jnp.roll(grid_field, -offset * width, axis=-1)
        summed = summed + weight * (shift_x + shift_y)
    return summed


def apply_ham(padded, potential, column_x):
    middle = padded[:, 2:-2]
    laplace = in_plane(middle, column_x, NX) - 30.0 * middle
    laplace = (
        laplace + 16.0 * (padded[:, 1:-3] + padded[:, 3:-1]) - (padded[:, :-4] + padded[:, 4:])
    )
    return -0.5 * STENCIL * laplace + potential[None] * middle


def extended(grid_field):
    return extended_2(grid_field, (("slab", 1),), 2)


def local(orbitals, potential):
    column_x = lax.iota(jnp.int32, orbitals.shape[2]) % NX
    section_one = (
        apply_ham(extended(orbitals), potential, column_x) - CENTER * orbitals
    ) / HALF_WIDTH
    filtered = (
        2.0
        * (apply_ham(extended(section_one), potential, column_x) - CENTER * section_one)
        / HALF_WIDTH
        - orbitals
    )
    applied = apply_ham(extended(filtered), potential, column_x)
    panel_rows = orbitals.shape[0]
    cell_count = orbitals.shape[1] * orbitals.shape[2]
    flat_filtered = filtered.reshape(panel_rows, cell_count)
    flat_applied = applied.reshape(panel_rows, cell_count)
    factor = 1.0 / (cell_count * lax.axis_size("slab"))
    contract_dims = (((1,), (1,)), ((), ()))
    panel_piece = lax.all_gather(flat_filtered, "band", axis=0, tiled=True)
    correlation_part = lax.dot_general(
        flat_filtered,
        panel_piece,
        contract_dims,
        precision=lax.Precision.HIGHEST,
        preferred_element_type=jnp.float32,
    )
    projected_part = lax.dot_general(
        flat_applied,
        panel_piece,
        contract_dims,
        precision=lax.Precision.HIGHEST,
        preferred_element_type=jnp.float32,
    )
    correlation, projected = (
        lax.psum_scatter(correlation_part * factor, "slab", scatter_dimension=1, tiled=True),
        lax.psum_scatter(projected_part * factor, "slab", scatter_dimension=1, tiled=True),
    )
    return (filtered, correlation, projected)


def solution(mesh):
    placed = (P("band", "slab", None), P("slab", None))
    return jax.shard_map(
        local,
        mesh=mesh,
        in_specs=placed,
        out_specs=(P("band", "slab", None), P("band", "slab"), P("band", "slab")),
        check_vma=False,
    )
```

profile of v0, /device:TPU:0, one launch (start us, length us, event | category | flops | bytes accessed | tf_op | source)
XLA Modules:
  0.0 435.8 jit_solution(524187664041806085)
XLA Ops:
  7.2 1.2 fusion.125
  8.4 1.6 collective-permute-start
  10.1 2.7 collective-permute-start.1
  12.8 3.5 fusion.113
  19.8 3.2 fusion.123
  28.1 10.4 %broadcast_multiply_fusion = (f32[24,12,2304]{2,0,1:T(8,128)S(1)}, f32[24,12,2304]{2,0,1:T(8,128)}) fusion(f32[24,12,2304]{2,0,1:T(8,128)S(1)} %copy-done, f32[12,2304]{1,0:T(8,128)S(1)} %copy-done.3, f32[24,14,2304]{2,0,1:T(8,128)S(1)} %constant_dynamic-update-slice_fusion.2, f32[24,14,2304]{2,0,1:T(8,128)S(1)} %get-tuple-element.81, ...), kind=kLoop, calls=%fused_computation.93 | loop fusion | flops 27869184 | bytes 50549760 | tf_op jit(solution)/shard_map/div | solution.py:59
  41.9 2.4 fusion.108
  44.3 3.2 fusion.111
  48.1 4.1 collective-permute-start.3
  52.4 9.4 %collective-permute-done.2 = f32[24,2,2304]{2,0,1:T(8,128)S(1)} collective-permute-done((f32[24,2,2304]{2,0,1:T(8,128)S(1)}, f32[24,2,2304]{2,0,1:T(8,128)S(1)}, u32[]{:S(2)}, u32[]{:S(2)}) %collective-permute-start.2) | collective-permute-done | bytes 442400 | tf_op jit(solution)/shard_map/ppermute | solution.py:21
  62.8 9.8 %fusion.18 = f32[24,12,2304]{2,0,1:T(8,128)S(1)} fusion(f32[24,12,2304]{2,0,1:T(8,128)S(1)} %copy-done, f32[24,12,2304]{2,0,1:T(8,128)S(1)} %get-tuple-element.3, f32[24,2,2304]{2,0,1:T(8,128)} %copy-done.5, f32[24,2,2304]{2,0,1:T(8,128)} %copy-done.4, f32[24,12,1]{2,0,1:T(8,128)S(1)} %get-tuple-element.52, f32[24,12,2303]{2,0,1:T(8,128)} %get-tuple-element.54, ...), kind=kLoop, calls=%fused_computation.26 | loop fusion | flops 31186944 | bytes 43471872 | tf_op jit(solution)/shard_map/sub | solution.py:63
  72.7 1.8 copy.13
  74.7 14.8 %collective-permute-start.5 = (f32[24,2,2304]{2,0,1:T(8,128)S(1)}, f32[24,2,2304]{2,0,1:T(8,128)S(1)}, u32[]{:S(2)}, u32[]{:S(2)}) collective-permute-start(f32[24,2,2304]{2,0,1:T(8,128)S(1)} %get-tuple-element.30), channel_id=1, source_target_pairs={{16,0},{32,16},{48,32},{64,48},{80,64},{96,80},{112,96},{0,112},{1... | collective-permute-start | bytes 1327112 | tf_op jit(solution)/shard_map/ppermute | solution.py:24
  89.9 0.9 fusion.89
  91.6 0.8 fusion.94
  94.2 2.3 fusion.88
  97.5 15.9 %fusion.7 = f32[12,3,8,2304]{3,2,1,0:T(8,128)} fusion(f32[24,12,2304]{2,0,1:T(8,128)S(1)} %fusion.18, f32[24,2,2304]{2,0,1:T(8,128)S(1)} %collective-permute-done.5, f32[24,2,2304]{2,0,1:T(8,128)S(1)} %collective-permute-done.4, f32[24,12,1]{2,0,1:T(8,128)S(1)} %get-tuple-element.26, f32[24,12,2303]{2,0,1:T(8,128)S(1)} %get-tuple-element.28, ...), kind=kLoop, calls=%fused_computation.15 | loop fusion | flops 28532736 | bytes 38163456
  113.4 3.5 copy.14
  116.8 196.2 %all-gather.2.cloned.1.call-done = f32[384,27648]{1,0:T(8,128)} async-done(((f32[24,27648]{1,0:T(8,128)}), f32[384,27648]{1,0:T(8,128)}) %all-gather.2.cloned.1.call-update) | async-done | bytes 42467344 | tf_op jit(solution)/shard_map/all_gather | solution.py:75
  313.1 39.1 %convolution_multiply_fusion = f32[24,384]{1,0:T(8,128)S(1)} fusion(f32[24,27648]{1,0:T(8,128)} %bitcast.16, f32[384,27648]{1,0:T(8,128)} %all-gather.2.cloned.1.call-done), kind=kOutput, calls=%fused_computation.94 | convolution fusion | flops 3057656832 | bytes 45158400 | tf_op jit(solution)/shard_map/dot_general | solution.py:83
  353.1 39.1 %convolution_multiply_fusion.1 = f32[24,384]{1,0:T(8,128)S(1)} fusion(f32[24,27648]{1,0:T(8,128)S(1)} %bitcast.15, f32[384,27648]{1,0:T(8,128)} %all-gather.2.cloned.1.call-done), kind=kOutput, calls=%fused_computation.95 | convolution fusion | flops 3057656832 | bytes 45158400 | tf_op jit(solution)/shard_map/dot_general | solution.py:76
  393.1 1.4 copy.12
  394.5 33.1 %reduce-scatter.7.cloned.1.call-done = f32[48,24]{1,0:T(8,128)} async-done(((f32[384,24]{1,0:T(8,128)}), f32[48,24]{1,0:T(8,128)}) %reduce-scatter.7.cloned.1.call-update) | async-done | bytes 4624
  427.7 1.4 copy.10
  (65 shorter events, 19.4 us)
Async XLA Ops:
  7.2 305.9 %all-gather.2.cloned.1.call-start = ((), (), s32[]{:S(2)}) async-start(), calls=%async_computation.2 | async-start | bytes 45121536 | tf_op jit(solution)/shard_map/all_gather | solution.py:75
  8.4 19.2 %collective-permute-start = (f32[24,2,2304]{2,0,1:T(8,128)S(1)}, f32[24,2,2304]{2,0,1:T(8,128)S(1)}, u32[]{:S(2)}, u32[]{:S(2)}) collective-permute-start(f32[24,2,2304]{2,0,1:T(8,128)S(1)} %get-tuple-element.83), channel_id=1, source_target_pairs={{0,16},{16,32},{32,48},{48,64},{64,80},{80,96},{96,112},{112,0},{1... | collective-permute-start | bytes 1327112 | tf_op jit(solution)/shard_map/ppermute | solution.py:21
  10.1 18.0 %collective-permute-start.1 = (f32[24,2,2304]{2,0,1:T(8,128)S(1)}, f32[24,2,2304]{2,0,1:T(8,128)S(1)}, u32[]{:S(2)}, u32[]{:S(2)}) collective-permute-start(f32[24,2,2304]{2,0,1:T(8,128)S(1)} %get-tuple-element.84), channel_id=1, source_target_pairs={{16,0},{32,16},{48,32},{64,48},{80,64},{96,80},{112,96},{0,112},{1... | collective-permute-start | bytes 1327112 | tf_op jit(solution)/shard_map/ppermute | solution.py:24
  12.8 3.6 copy-start
  19.8 6.3 %copy-start.3 = (f32[12,2304]{1,0:T(8,128)S(1)}, f32[12,2304]{1,0:T(8,128)}, u32[]{:S(2)}) copy-start(f32[12,2304]{1,0:T(8,128)} %param.3) | copy-start | bytes 331780
  48.0 13.8 %collective-permute-start.2 = (f32[24,2,2304]{2,0,1:T(8,128)S(1)}, f32[24,2,2304]{2,0,1:T(8,128)S(1)}, u32[]{:S(2)}, u32[]{:S(2)}) collective-permute-start(f32[24,2,2304]{2,0,1:T(8,128)S(1)} %get-tuple-element.55), channel_id=1, source_target_pairs={{0,16},{16,32},{32,48},{48,64},{64,80},{80,96},{96,112},{112,0},{1... | collective-permute-start | bytes 1327112 | tf_op jit(solution)/shard_map/ppermute | solution.py:21
  48.1 13.7 %collective-permute-start.3 = (f32[24,2,2304]{2,0,1:T(8,128)S(1)}, f32[24,2,2304]{2,0,1:T(8,128)S(1)}, u32[]{:S(2)}, u32[]{:S(2)}) collective-permute-start(f32[24,2,2304]{2,0,1:T(8,128)S(1)} %get-tuple-element.56), channel_id=1, source_target_pairs={{16,0},{32,16},{48,32},{64,48},{80,64},{96,80},{112,96},{0,112},{1... | collective-permute-start | bytes 1327112 | tf_op jit(solution)/shard_map/ppermute | solution.py:24
  61.8 0.8 copy-start.4
  61.8 1.0 copy-start.5
  72.7 24.8 %copy-start.1 = (f32[24,12,2304]{2,0,1:T(8,128)}, f32[24,12,2304]{2,0,1:T(8,128)S(1)}, u32[]{:S(2)}) copy-start(f32[24,12,2304]{2,0,1:T(8,128)S(1)} %fusion.18) | copy-start | bytes 7962628
  74.5 318.6 %reduce-scatter.9.cloned.1.call-start = ((), (), s32[]{:S(2)}) async-start(), calls=%async_computation.4 | async-start | bytes 221184
  74.6 22.1 %collective-permute-start.4 = (f32[24,2,2304]{2,0,1:T(8,128)S(1)}, f32[24,2,2304]{2,0,1:T(8,128)S(1)}, u32[]{:S(2)}, u32[]{:S(2)}) collective-permute-start(f32[24,2,2304]{2,0,1:T(8,128)S(1)} %get-tuple-element.29), channel_id=1, source_target_pairs={{0,16},{16,32},{32,48},{48,64},{64,80},{80,96},{96,112},{112,0},{1... | collective-permute-start | bytes 1327112 | tf_op jit(solution)/shard_map/ppermute | solution.py:21
  74.7 22.8 %collective-permute-start.5 = (f32[24,2,2304]{2,0,1:T(8,128)S(1)}, f32[24,2,2304]{2,0,1:T(8,128)S(1)}, u32[]{:S(2)}, u32[]{:S(2)}) collective-permute-start(f32[24,2,2304]{2,0,1:T(8,128)S(1)} %get-tuple-element.30), channel_id=1, source_target_pairs={{16,0},{32,16},{48,32},{64,48},{80,64},{96,80},{112,96},{0,112},{1... | collective-permute-start | bytes 1327112 | tf_op jit(solution)/shard_map/ppermute | solution.py:24
  313.1 40.0 %copy-start.2 = (f32[12,3,8,2304]{3,2,0,1:T(8,128)S(1)}, f32[12,3,8,2304]{3,2,0,1:T(8,128)}, u32[]{:S(2)}) copy-start(f32[12,3,8,2304]{3,2,0,1:T(8,128)} %copy.13) | copy-start | bytes 7962628
  353.1 74.6 %reduce-scatter.7.cloned.1.call-start = ((), (), s32[]{:S(2)}) async-start(), calls=%async_computation.3 | async-start | bytes 221184
Sparse Core Ops, SparseCore 0:
  74.6 238.4 all-gather.1
  353.2 34.4 reduce-scatter.8
  393.2 34.4 reduce-scatter.6
where the time goes:
time: 442 us; the launch traced here: 436 us
  waiting for transfers between devices  240 us (54%)
  matrix products  78.3 us (18%)
  local copies, waits for them, and re-layouts  44 us (10%)
  other arithmetic  36.2 us (8%)
  starting transfers between devices  23.5 us (5%)
  between operations  14.3 us (3%)
    all_gather x1, waiting for transfers between devices, local(): panel_piece = lax.all_gather(flat_filtered, 'band', axis=0, tiled=True)  196 us
    dot_general x1, matrix products, local(): lax.dot_general(flat_applied, panel_piece, contract_dims, precision=lax.P...  39.1 us
    dot_general x1, matrix products, local(): lax.dot_general(flat_filtered, panel_piece, contract_dims, precision=lax....  39.1 us
    unnamed x5, waiting for transfers between devices  33.2 us
    ppermute x3, starting transfers between devices, extended_2(): lax.ppermute(lax.slice_in_dim(block, 0, width, axis=dim), axis, backward)  21.6 us
    unnamed x1, other arithmetic  15.9 us
    slice x12, local copies, waits for them, and re-layouts, in_plane(): jnp.roll(grid_field, -offset, axis=-1)  12.1 us
    slice x12, local copies, waits for them, and re-layouts, in_plane(): shift_y = jnp.roll(grid_field, -offset * width, axis=-1)  10.9 us
  transfers between devices with their start and end apart: 9, of which 4 were waited for; matrix products, arithmetic and copies ran while one was open for 19% of the time, Pallas kernels for 0%

commit v1 on v0

v1 whole, which is shorter than its diff:
```python
import jax
import jax.numpy as jnp
from jax import lax
from jax.experimental import pallas as pl
from jax.experimental.pallas import tpu as pltpu
from jax.sharding import PartitionSpec as P

NX = 48
NXY = 2304
ORB = 24
PLANES = 12
CHIPS = 8
SLABS = 8
HALF = NXY // 2
CHUNK = 384
CELLS = 221184

SPACING = 0.32
STENCIL = 1.0 / (12.0 * SPACING * SPACING)
CENTER = 38.0
HALF_WIDTH = 42.0
NEAR = -8.0 * STENCIL / HALF_WIDTH
FAR = 0.5 * STENCIL / HALF_WIDTH
MESH = pl.DeviceIdType.MESH

PEERS = ((1, 0), (0, 1), (1, 2), (0, 3), (1, 1), (0, 2), (1, 3))


def dot_nt(a, b):
    return lax.dot_general(a, b, (((1,), (1,)), ((), ())), preferred_element_type=jnp.float32)


def halves(a):
    high = a.astype(jnp.bfloat16)
    return high, (a - high.astype(jnp.float32)).astype(jnp.bfloat16)


def kernel(
    orb_hbm, pot_ref, filt_hbm, corr_ref, proj_ref,
    O, V_in, W, S, F, A, RF, RA, G, R1, B2, R2,
    load_sem, out_sem, halo_s, halo_r, pot_s, pot_r, swap_s, swap_r, own_sem, fwd_s, fwd_r,
    r1_s, r1_r, r2_s, r2_r,
):
    band, slab = lax.axis_index("band"), lax.axis_index("slab")
    chip, core = band // 2, band % 2
    z_hi, y = chip // 4, chip % 4

    def chip_at(offset):
        return ((z_hi + offset[0]) % 2) * 4 + (y + offset[1]) % 4

    def to_band(b):
        return {"band": b, "slab": slab}

    def to_slab(s):
        return {"band": band, "slab": s}

    load = pltpu.make_async_copy(orb_hbm, O.at[pl.ds(6, PLANES)], load_sem)
    load.start()

    up, down = (slab + 1) % SLABS, (slab + SLABS - 1) % SLABS
    partners = [to_band(chip_at(o) * 2 + core) for o in PEERS]
    partners.append(to_band(chip * 2 + 1 - core))
    partners += [to_slab((slab + d) % SLABS) for d in range(1, SLABS)]
    barrier = pltpu.get_barrier_semaphore()
    for partner in partners:
        pl.semaphore_signal(barrier, inc=1, device_id=partner, device_id_type=MESH)
    pl.semaphore_wait(barrier, len(partners))

    sends = []

    def send(src, dst, s_sem, r_sem, where):
        copy = pltpu.make_async_remote_copy(
            src_ref=src, dst_ref=dst, send_sem=s_sem, recv_sem=r_sem,
            device_id=where, device_id_type=MESH,
        )
        copy.start()
        sends.append(copy)
        return copy

    pots = [
        send(pot_ref.at[pl.ds(4, 8)], V_in.at[0], pot_s.at[0], pot_r.at[0], to_slab(up)),
        send(pot_ref.at[pl.ds(0, 8)], V_in.at[1], pot_s.at[1], pot_r.at[1], to_slab(down)),
    ]
    load.wait()
    halos = []
    for t in range(3):
        halos.append((
            send(O.at[pl.ds(16 - 2 * t, 2)], O.at[pl.ds(4 - 2 * t, 2)],
                 halo_s.at[0, t], halo_r.at[0, t], to_slab(up)),
            send(O.at[pl.ds(6 + 2 * t, 2)], O.at[pl.ds(18 + 2 * t, 2)],
                 halo_s.at[1, t], halo_r.at[1, t], to_slab(down)),
        ))

    def fill(z, row):
        weight = (row + (45.0 * STENCIL - CENTER)) * (1.0 / HALF_WIDTH)
        W[z + 4] = jnp.broadcast_to(weight, (8, NXY))

    for z in range(PLANES):
        fill(z, pot_ref[z : z + 1, :])

    x_at = (lax.broadcasted_iota(jnp.int32, (8, CHUNK + 256), 1) + 16) % NX

    def stage(src, src_off, first, count, second, emit):
        total = count if second is None else 2 * count

        def body(i, carry):
            p = i // 3
            z = first + p
            if second is not None:
                z = z + (p // count) * (second - first - count)
            rows = pl.ds(pl.multiple_of((i % 3) * 8, 8), 8)
            at = z + src_off
            for g in range(NXY // CHUNK):
                lanes = pl.ds(g * CHUNK, CHUNK)
                lo, hi = (g * CHUNK - 128) % NXY, (g * CHUNK + CHUNK) % NXY
                v = src[at, rows, lanes]
                wide = jnp.concatenate(
                    [src[at, rows, pl.ds(lo, 128)], v, src[at, rows, pl.ds(hi, 128)]], axis=1
                )
                size = CHUNK + 256

                def cut(a, shift):
                    return pltpu.roll(a, shift % size, 1)[:, 128 : 128 + CHUNK]

                before, after = pltpu.roll(wide, NX, 1), pltpu.roll(wide, size - NX, 1)
                near = before[:, 128 : 128 + CHUNK] + after[:, 128 : 128 + CHUNK]
                near = near + cut(jnp.where(x_at == 0, before, wide), -1)
                near = near + cut(jnp.where(x_at == NX - 1, after, wide), 1)
                near = near + (src[at - 1, rows, lanes] + src[at + 1, rows, lanes])
                far = cut(wide, 2 * NX) + cut(wide, -2 * NX)
                far = far + cut(jnp.where(x_at < 2, before, wide), -2)
                far = far + cut(jnp.where(x_at >= NX - 2, after, wide), 2)
                far = far + (src[at - 2, rows, lanes] + src[at + 2, rows, lanes])
                h = NEAR * near + FAR * far + W[z + 4, :, lanes] * v
                emit(z, rows, lanes, h, v)
            return carry

        lax.fori_loop(0, 3 * total, body, 0)

    def emit_s(z, rows, lanes, h, v):
        S[z + 4, rows, lanes] = h

    def emit_f(z, rows, lanes, h, v):
        F[z + 2, rows, lanes] = 2.0 * h - O[z + 6, rows, lanes]

    def emit_a(z, rows, lanes, h, v):
        A[z, rows, lanes] = HALF_WIDTH * h + CENTER * v

    def stage_s(first, count, second=None):
        stage(O, 6, first, count, second, emit_s)

    def stage_f(first, count, second=None):
        stage(S, 4, first, count, second, emit_f)

    def stage_a(first, count, second=None):
        stage(F, 2, first, count, second, emit_a)

    def swap(kind, q):
        src, off = ((F, 2), (A, 0))[kind]

        def part(c):
            lanes = pl.ds(pl.multiple_of((c % 2) * HALF, 128), HALF)
            return src.at[4 * q + c // 2 + off, :, lanes]

        dst = RF.at[q, chip, core] if kind == 0 else RA.at[q, chip]
        copies = []
        for d, o in enumerate(PEERS):
            c = chip_at(o)
            copies.append(
                send(part(c), dst, swap_s.at[kind, q, d], swap_r.at[kind, q, d], to_band(c * 2 + core))
            )
        own = pltpu.make_async_copy(part(chip), dst, own_sem.at[kind, q])
        own.start()
        return copies, own

    def swap_wait(copies, own):
        own.wait()
        for copy in copies:
            copy.wait_recv()

    def forward(q):
        piece = RF.at[q, :, core]
        return send(piece, piece, fwd_s.at[q], fwd_r.at[q], to_band(chip * 2 + 1 - core))

    def gram(kind, q, start):
        def body(k, carry):
            lanes = pl.ds(pl.multiple_of(k * CHUNK, 128), CHUNK)
            f_high, f_low = halves(RF[q, :, :, :, lanes].reshape(2 * CHIPS * ORB, CHUNK))
            rows = RF[q, :, core, :, lanes] if kind == 0 else RA[q, :, :, lanes]
            high, low = halves(rows.reshape(CHIPS * ORB, CHUNK))
            part = dot_nt(high, f_high) + (dot_nt(high, f_low) + dot_nt(low, f_high))
            G[kind] = G[kind] + part.reshape(CHIPS, ORB, 2 * CHIPS * ORB)
            return carry

        if start:
            G[kind] = jnp.zeros((CHIPS, ORB, 2 * CHIPS * ORB), jnp.float32)
        lax.fori_loop(0, HALF // CHUNK, body, 0)

    def reduce_band(kind):
        copies = []
        for d, o in enumerate(PEERS):
            c = chip_at(o)
            copies.append(
                send(G.at[kind, c], R1.at[kind, d], r1_s.at[kind, d], r1_r.at[kind, d],
                     to_band(c * 2 + core))
            )
        return copies

    def reduce_slab(kind, arrived):
        for copy in arrived:
            copy.wait_recv()
        rows = G[kind, chip]
        for d in range(len(PEERS)):
            rows = rows + R1[kind, d]
        for s in range(SLABS):
            B2[kind, s] = pltpu.roll(rows, (-NX * s) % (NX * SLABS), 1)[:, :128]
        copies = []
        for d in range(1, SLABS):
            s = (slab + d) % SLABS
            copies.append(
                send(B2.at[kind, s], R2.at[kind, d - 1], r2_s.at[kind, d - 1], r2_r.at[kind, d - 1],
                     to_slab(s))
            )
        return copies

    def finish(kind, arrived, out):
        for copy in arrived:
            copy.wait_recv()
        block = B2[kind, slab]
        for d in range(SLABS - 1):
            block = block + R2[kind, d]
        out[...] = block[:, :NX] * (1.0 / CELLS)

    stage_s(2, 8)
    stage_f(4, 4)
    f1 = swap(0, 1)

    for copy in halos[0]:
        copy.wait_recv()
    stage_s(0, 2, 10)
    stage_f(2, 2, 8)
    stage_a(4, 4)
    a1 = swap(1, 1)

    for copy in pots:
        copy.wait_recv()
    for n in range(4):
        fill(n - 4, V_in[0, 4 + n : 5 + n, :])
        fill(12 + n, V_in[1, n : n + 1, :])
    for copy in halos[1]:
        copy.wait_recv()
    stage_s(-2, 2, 12)
    stage_f(0, 2, 10)
    f0, f2 = swap(0, 0), swap(0, 2)
    store = pltpu.make_async_copy(F.at[pl.ds(2, PLANES)], filt_hbm, out_sem)
    store.start()

    swap_wait(*f1)
    w1 = forward(1)
    for copy in halos[2]:
        copy.wait_recv()
    stage_s(-4, 2, 14)
    stage_f(-2, 2, 12)
    stage_a(0, 4, 8)
    a0, a2 = swap(1, 0), swap(1, 2)

    w1.wait_recv()
    gram(0, 1, True)
    swap_wait(*a1)
    gram(1, 1, True)
    swap_wait(*f0)
    w0 = forward(0)
    swap_wait(*f2)
    w2 = forward(2)
    w0.wait_recv()
    gram(0, 0, False)
    w2.wait_recv()
    gram(0, 2, False)
    c1 = reduce_band(0)
    swap_wait(*a0)
    gram(1, 0, False)
    c2 = reduce_slab(0, c1)
    swap_wait(*a2)
    gram(1, 2, False)
    p1 = reduce_band(1)
    finish(0, c2, corr_ref)
    p2 = reduce_slab(1, p1)
    finish(1, p2, proj_ref)
    for copy in sends:
        copy.wait_send()
    store.wait()


def local(orbitals, potential):
    f32 = jnp.float32
    dma = pltpu.SemaphoreType.DMA
    peers = len(PEERS)
    filtered, correlation, projected = pl.pallas_call(
        kernel,
        out_shape=(
            jax.ShapeDtypeStruct((PLANES, ORB, NXY), f32),
            jax.ShapeDtypeStruct((ORB, NX), f32),
            jax.ShapeDtypeStruct((ORB, NX), f32),
        ),
        in_specs=[pl.BlockSpec(memory_space=pl.ANY), pl.BlockSpec(memory_space=pltpu.VMEM)],
        out_specs=(
            pl.BlockSpec(memory_space=pl.ANY),
            pl.BlockSpec(memory_space=pltpu.VMEM),
            pl.BlockSpec(memory_space=pltpu.VMEM),
        ),
        scratch_shapes=[
            pltpu.VMEM((PLANES + 12, ORB, NXY), f32),
            pltpu.VMEM((2, 8, NXY), f32),
            pltpu.VMEM((PLANES + 8, 8, NXY), f32),
            pltpu.VMEM((PLANES + 8, ORB, NXY), f32),
            pltpu.VMEM((PLANES + 4, ORB, NXY), f32),
            pltpu.VMEM((PLANES, ORB, NXY), f32),
            pltpu.VMEM((3, CHIPS, 2, ORB, HALF), f32),
            pltpu.VMEM((3, CHIPS, ORB, HALF), f32),
            pltpu.VMEM((2, CHIPS, ORB, 2 * CHIPS * ORB), f32),
            pltpu.VMEM((2, peers, ORB, 2 * CHIPS * ORB), f32),
            pltpu.VMEM((2, SLABS, ORB, 128), f32),
            pltpu.VMEM((2, SLABS - 1, ORB, 128), f32),
            dma, dma,
            dma((2, 3)), dma((2, 3)),
            dma((2,)), dma((2,)),
            dma((2, 3, peers)), dma((2, 3, peers)),
            dma((2, 3)),
            dma((3,)), dma((3,)),
            dma((2, peers)), dma((2, peers)),
            dma((2, SLABS - 1)), dma((2, SLABS - 1)),
        ],
        compiler_params=pltpu.CompilerParams(
            collective_id=0, has_side_effects=True, vmem_limit_bytes=56 << 20
        ),
        cost_estimate=pl.CostEstimate(
            flops=3_500_000_000, bytes_accessed=6_000_000, transcendentals=0
        ),
    )(jnp.transpose(orbitals, (1, 0, 2)), potential)
    return jnp.transpose(filtered, (1, 0, 2)), correlation, projected


def solution(mesh):
    return jax.shard_map(
        local,
        mesh=mesh,
        in_specs=(P("band", "slab", None), P("slab", None)),
        out_specs=(P("band", "slab", None), P("band", "slab"), P("band", "slab")),
        check_vma=False,
    )
```

time: 442 us -> 137 us (0.31); the launches traced: 436 us -> 137 us
  waiting for transfers between devices: 240 us -> 0 us
  Pallas kernels: 0 us -> 132 us
  matrix products: 78.3 us -> 0 us
  local copies, waits for them, and re-layouts: 44 us -> 4.64 us
  other arithmetic: 36.2 us -> 0 us
  starting transfers between devices: 23.5 us -> 0 us
  between operations: 14.3 us -> 0.66 us
    all_gather x1 -> x0, waiting for transfers between devices: 196 us -> none  [local(): panel_piece = lax.all_gather(flat_filtered, 'band', axis=0, tiled=True)]
    pallas_call x0 -> x1, Pallas kernels: none -> 132 us  [local(): pl.pallas_call(kernel, out_shape=(jax.ShapeDtypeStruct((PLANES, ORB, NXY)...]
    dot_general x2 -> x0, matrix products: 78.3 us -> none  [the longest x1 39.1 us: local(): lax.dot_general(flat_applied, panel_piece, contract_dims, precision=lax.P...]
    unnamed x5 -> x0, waiting for transfers between devices: 33.2 us -> none
    slice x39 -> x0, local copies, waits for them, and re-layouts: 32.8 us -> none  [the longest x12 12.1 us: in_plane(): jnp.roll(grid_field, -offset, axis=-1)]
    ppermute x6 -> x0, starting transfers between devices: 23.4 us -> none  [the longest x3 21.6 us: extended_2(): lax.ppermute(lax.slice_in_dim(block, 0, width, axis=dim), axis, backward)]
    unnamed x1 -> x0, other arithmetic: 15.9 us -> none
    div x1 -> x0, other arithmetic: 10.4 us -> none  [local(): (apply_ham(extended(orbitals), potential, column_x) - CENTER * orbitals)...]
  transfers between devices with their start and end apart: 9 -> 0, of which waited for: 4 -> 0; matrix products, arithmetic and copies ran while one was open for 19% -> 0% of each run, Pallas kernels for 0% -> 0%
where the time goes in v1:
time: 137 us
  Pallas kernels  132 us (96%)
  local copies, waits for them, and re-layouts  4.64 us (3%)
    pallas_call x1, Pallas kernels, local(): pl.pallas_call(kernel, out_shape=(jax.ShapeDtypeStruct((PLANES, ORB, NXY)...  132 us
    unnamed x7, local copies, waits for them, and re-layouts  4.64 us

profile of v1, /device:TPU:0, one launch (start us, length us, event | category | flops | bytes accessed | tf_op | source)
XLA Modules:
  0.0 136.8 jit_solution(18430090107163939541)
XLA Ops:
  0.6 131.5 %shard_map.49 = (f32[12,24,2304]{2,1,0:T(8,128)}, f32[24,48]{1,0:T(8,128)}, f32[24,48]{1,0:T(8,128)}) custom-call(f32[12,24,2304]{2,1,0:T(8,128)} %bitcast.3, f32[12,2304]{1,0:T(8,128)} %pot_ref.1), custom_call_target="tpu_custom_call" | custom-call | flops 3500000000 | bytes 6000000 | tf_op jit(solution)/shard_map/pallas_call | solution.py:298
  132.2 0.0 copy-start.1
  132.2 0.0 copy-start
  132.2 3.4 %copy.8 = f32[24,12,2304]{2,0,1:T(8,128)} copy(f32[24,12,2304]{2,0,1:T(8,128)} %bitcast.2) | data formatting | bytes 5308416
  135.6 0.0 copy-done.1
  135.6 0.6 copy.9
  136.2 0.0 copy-done
  136.2 0.6 copy.10
Async XLA Ops:
  132.2 3.5 %copy-start.1 = (f32[24,48]{1,0:T(8,128)S(1)}, f32[24,48]{1,0:T(8,128)}, u32[]{:S(2)}) copy-start(f32[24,48]{1,0:T(8,128)} %get-tuple-element.13) | copy-start | bytes 13828
  132.2 4.0 %copy-start = (f32[24,48]{1,0:T(8,128)S(1)}, f32[24,48]{1,0:T(8,128)}, u32[]{:S(2)}) copy-start(f32[24,48]{1,0:T(8,128)} %get-tuple-element.14) | copy-start | bytes 13828

commit v2 on v0

v2 whole, which is shorter than its diff:
```python
import jax
import jax.numpy as jnp
import ml_dtypes
import numpy as np
from jax import lax
from jax.experimental import pallas as pl
from jax.experimental.pallas import tpu as pltpu
from jax.sharding import PartitionSpec as P

NX = 48
NXY = 2304
ORB = 24
PLANES = 12
SLABS = 8
HALF = NXY // 2
CHUNK = 384
CELLS = 221184

SPACING = 0.32
STENCIL = 1.0 / (12.0 * SPACING * SPACING)
CENTER = 38.0
HALF_WIDTH = 42.0
NEAR = -0.5 * STENCIL / HALF_WIDTH
MESH = pl.DeviceIdType.MESH

CHUNK_BASE = (4, 2, 0)
CHUNK_STRIDE = (0, 4, 8)
PEERS = (1, 3, 2)
HALF_ORB = 192
ROWS = 96


def plane_table():
    table = np.zeros((3, 512, 256), np.float32)
    for r in range(3):
        for n in range(256):
            cell = 256 * r + n
            row, x = cell // NX, cell % NX
            for offset, weight in ((1, 16.0), (2, -1.0), (-1, 16.0), (-2, -1.0)):
                table[r, row * NX + (x + offset) % NX - 256 * r + 128, n] += weight
                table[r, n + 128 + offset * NX, n] += weight
    return table.astype(ml_dtypes.bfloat16)


def dot_nt(a, b):
    return lax.dot_general(a, b, (((1,), (1,)), ((), ())), preferred_element_type=jnp.float32)


def halves(a):
    high = a.astype(jnp.bfloat16)
    return high, (a - high.astype(jnp.float32)).astype(jnp.bfloat16)


def kernel(
    orb_hbm, pot_ref, table_hbm, filt_hbm, corr_ref, proj_ref,
    O, T, V_in, W, S, F, A, RF, RA, RA_far, G, G_far, R1, XB, XR, B2, R2,
    load_sem, table_sem, out_sem, halo_s, halo_r, pot_s, pot_r, swap_s, swap_r, own_sem, fwd_s, fwd_r,
    far_s, far_r, early_s, early_r, r1_s, r1_r, x_s, x_r, r2_s, r2_r,
):
    band, slab = lax.axis_index("band"), lax.axis_index("slab")
    chip, core = band // 2, band % 2
    z_hi, y = chip // 4, chip % 4

    def to_band(z, row, side):
        return {"band": z * 8 + row * 2 + side, "slab": slab}

    def to_slab(s):
        return {"band": band, "slab": s}

    load = pltpu.make_async_copy(orb_hbm, O.at[pl.ds(6, PLANES)], load_sem)
    load.start()
    table_load = pltpu.make_async_copy(table_hbm, T, table_sem)
    table_load.start()

    up, down = (slab + 1) % SLABS, (slab + SLABS - 1) % SLABS
    partners = [to_band(z_hi, (y + d) % 4, core) for d in PEERS]
    partners.append(to_band(z_hi, y, 1 - core))
    partners += [to_band(1 - z_hi, row, side) for row in range(4) for side in range(2)]
    partners += [to_slab((slab + d) % SLABS) for d in range(1, SLABS)]
    barrier = pltpu.get_barrier_semaphore()
    for partner in partners:
        pl.semaphore_signal(barrier, inc=1, device_id=partner, device_id_type=MESH)

    sends = []

    def send(src, dst, s_sem, r_sem, where):
        copy = pltpu.make_async_remote_copy(
            src_ref=src, dst_ref=dst, send_sem=s_sem, recv_sem=r_sem,
            device_id=where, device_id_type=MESH,
        )
        copy.start()
        sends.append(copy)
        return copy

    def fill(z, row):
        weight = (row + (45.0 * STENCIL - CENTER)) * (1.0 / HALF_WIDTH)
        W[z + 4] = jnp.broadcast_to(weight, (8, NXY))

    for z in range(PLANES):
        fill(z, pot_ref[z : z + 1, :])

    table_load.wait()
    load.wait()

    def stage(src, src_off, starts, emit):
        count = 4 // len(starts)

        def planes(ref, off, rows, lanes):
            parts = [ref[pl.ds(z + off, count), rows, lanes] for z in starts]
            return parts[0] if len(parts) == 1 else jnp.concatenate(parts, axis=0)

        everything = slice(None)

        def body(i, carry):
            for r in range(3):
                base = i * 768 + 256 * r
                lanes = pl.ds(pl.multiple_of(base, 128), 256)
                left = pl.ds(pl.multiple_of((base + NXY - 128) % NXY, 128), 128)
                right = pl.ds(pl.multiple_of((base + 256) % NXY, 128), 128)
                v = planes(src, src_off, everything, lanes)
                wide = jnp.concatenate(
                    [planes(src, src_off, everything, left), v, planes(src, src_off, everything, right)],
                    axis=2,
                ).reshape(4 * ORB, 512)
                flat = jnp.dot(
                    jnp.concatenate(halves(wide), axis=0), T[r], preferred_element_type=jnp.float32
                )
                lap = (flat[: 4 * ORB] + flat[4 * ORB :]).reshape(4, ORB, 256)
                near = planes(src, src_off - 1, everything, lanes) + planes(src, src_off + 1, everything, lanes)
                far = planes(src, src_off - 2, everything, lanes) + planes(src, src_off + 2, everything, lanes)
                weight = planes(W, 4, everything, lanes)
                weight = jnp.concatenate([weight, weight, weight], axis=1)
                emit(lanes, NEAR * (lap + (16.0 * near - far)) + weight * v, v)
            return carry

        lax.fori_loop(0, 3, body, 0)

    def put(ref, off, starts, lanes, value):
        count = 4 // len(starts)
        for n, z in enumerate(starts):
            ref[pl.ds(z + off, count), :, lanes] = value[n * count : (n + 1) * count]

    def stage_s(*starts):
        def emit(lanes, h, v):
            put(S, 4, starts, lanes, h)

        stage(O, 6, starts, emit)

    def stage_f(*starts):
        count = 4 // len(starts)

        def emit(lanes, h, v):
            old = jnp.concatenate([O[pl.ds(z + 6, count), :, lanes] for z in starts], axis=0)
            put(F, 2, starts, lanes, 2.0 * h - old)

        stage(S, 4, starts, emit)

    def stage_a(*starts):
        def emit(lanes, h, v):
            put(A, 0, starts, lanes, HALF_WIDTH * h + CENTER * v)

        stage(F, 2, starts, emit)

    first = z_hi == 0

    def across(slot, row, piece):
        dst = RA_far.at[row] if slot == 3 else RF.at[slot, 1, row, core]
        return pltpu.make_async_remote_copy(
            src_ref=piece, dst_ref=dst,
            send_sem=far_s.at[slot, row], recv_sem=far_r.at[slot, row],
            device_id=to_band(1 - z_hi, y, core), device_id_type=MESH,
        )

    def sends_across(slot):
        return first if slot in (0, 3) else jnp.logical_not(first)

    def takes_across(slot):
        return jnp.logical_not(first) if slot in (0, 3) else first

    def landed(slot, row):
        return RA.at[0, row] if slot == 3 else RF.at[slot, 0, row, core]

    def swap(kind, q):
        src, off = ((F, 2), (A, 0))[kind]

        def part(row, n):
            plane = CHUNK_BASE[q] + row + CHUNK_STRIDE[q] * (row // 2)
            return src.at[plane + off, :, pl.ds(n * HALF, HALF)]

        def place(n):
            lanes = pl.ds(n * HALF, HALF)
            return RF.at[q, 0, y, core, :, lanes] if kind == 0 else RA.at[q, y, :, lanes]

        copies = []
        for n in range(2):
            for d in PEERS:
                row = (y + d) % 4
                copies.append(
                    send(part(row, n), place(n), swap_s.at[kind, q, d - 1, n], swap_r.at[kind, q, d - 1, n],
                         to_band(z_hi, row, core))
                )
        for n in range(2):
            own = pltpu.make_async_copy(part(y, n), place(n), own_sem.at[kind, q, n])
            own.start()
            copies.append(own)
        if kind == 0 or q == 0:
            slot = 3 if kind else q

            @pl.when(sends_across(slot))
            def _():
                plane = CHUNK_BASE[q] + y + CHUNK_STRIDE[q] * (y // 2)
                across(slot, y, src.at[plane + off]).start()

        return copies

    def swap_wait(copies):
        for copy in copies[:-2]:
            copy.wait_recv()
        for own in copies[-2:]:
            own.wait()

    def forward(q, half):
        piece = RF.at[q, half, :, core]
        return pltpu.make_async_remote_copy(
            src_ref=piece, dst_ref=piece, send_sem=fwd_s.at[q, half], recv_sem=fwd_r.at[q, half],
            device_id=to_band(z_hi, y, 1 - core), device_id_type=MESH,
        )

    def pass_on(slot, copies):
        for n, d in enumerate(PEERS):
            copies[n].wait_recv()
            copies[n + 3].wait_recv()

            @pl.when(sends_across(slot))
            def _():
                row = (y + 4 - d) % 4
                across(slot, row, landed(slot, row)).start()

        for own in copies[-2:]:
            own.wait()
        if slot < 3:
            forward(slot, 0).start()

    def wait_across(slot):
        for row in range(4):
            across(slot, row, landed(slot, row)).wait_recv()

    def pass_far(q):
        @pl.when(first)
        def _():
            wait_across(q)
            forward(q, 1).start()

    def gram(q, half, columns, f_rows, a_rows):
        def body(k, carry):
            lanes = pl.ds(pl.multiple_of(k * CHUNK, 128), CHUNK)
            f_high, f_low = halves(RF[q, columns, :, :, :, lanes].reshape(HALF_ORB, CHUNK))
            rows = jnp.concatenate([RF[q, f_rows, :, core, :, lanes], a_rows[:, :, lanes]], axis=0)
            high, low = halves(rows.reshape(2 * ROWS, CHUNK))
            both = dot_nt(jnp.concatenate([high, low], axis=0), f_high)
            part = (both[: 2 * ROWS] + both[2 * ROWS :]) + dot_nt(high, f_low)
            G[half] = G[half] + part.reshape(2, ROWS, HALF_ORB)
            return carry

        lax.fori_loop(0, NXY // CHUNK, body, 0)

    def gram_own(q):
        gram(q, 0, 0, 0, RA.at[q])

    def gram_far(q):
        @pl.when(first)
        def _():
            forward(q, 1).wait_recv()
            gram(q, 1, 1, 0, RA.at[q])

    def early():
        return pltpu.make_async_remote_copy(
            src_ref=G.at[1], dst_ref=G_far, send_sem=early_s, recv_sem=early_r,
            device_id=to_band(1 - z_hi, y, core), device_id_type=MESH,
        )

    def panel(row):
        return G.at[:, :, pl.ds(pl.multiple_of(row * ORB, 8), ORB)]

    def cross(row, side):
        index = row * 2 + side
        return pltpu.make_async_remote_copy(
            src_ref=XB.at[index], dst_ref=XR.at[y * 2 + core],
            send_sem=x_s.at[index], recv_sem=x_r.at[y * 2 + core],
            device_id=to_band(1 - z_hi, row, side), device_id_type=MESH,
        )

    def cross_from(index):
        return pltpu.make_async_remote_copy(
            src_ref=XB.at[index], dst_ref=XR.at[index],
            send_sem=x_s.at[index], recv_sem=x_r.at[index],
            device_id=to_band(1 - z_hi, index // 2, index % 2), device_id_type=MESH,
        )

    def reduce_band():
        copies = []
        for d in PEERS:
            row = (y + d) % 4
            copies.append(
                send(panel(row), R1.at[d - 1], r1_s.at[d - 1], r1_r.at[d - 1], to_band(z_hi, row, core))
            )

        @pl.when(first)
        def _():
            for kind in range(2):
                block = jnp.concatenate(
                    [G[1, kind], jnp.zeros((128 - ROWS, HALF_ORB), jnp.float32)], axis=0
                )
                XB[:, kind] = jnp.transpose(block).reshape(8, ORB, 128)
            for row in range(4):
                for side in range(2):
                    cross(row, side).start()

        return copies

    lane = lax.broadcasted_iota(jnp.int32, (ORB, 128), 1)

    def lanes_from(value, start):
        return pltpu.roll(value, (-start) % value.shape[1], 1)[:, :128]

    def reduce_slab(arrived):
        for copy in arrived:
            copy.wait_recv()
        mine = pl.ds(pl.multiple_of(y * ORB, 8), ORB)

        def rows_of(half, kind):
            rows = G[half, kind, mine]
            for d in range(len(PEERS)):
                rows = rows + R1[d, half, kind]
            return jnp.concatenate([rows, jnp.zeros((ORB, 64), jnp.float32)], axis=1)

        @pl.when(first)
        def _():
            for kind in range(2):
                own, other = rows_of(0, kind), rows_of(1, kind)
                for s in range(4):
                    B2[s, kind] = lanes_from(own, NX * s)
                    B2[s + 4, kind] = lanes_from(other, NX * s)

        @pl.when(jnp.logical_not(first))
        def _():
            for index in range(8):
                cross_from(index).wait_recv()
            for kind in range(2):
                own = rows_of(0, kind)
                sides = []
                for side in range(2):
                    total = XR[side, kind]
                    for row in range(1, 4):
                        total = total + XR[2 * row + side, kind]
                    sides.append(total)
                for s in range(4):
                    even = lanes_from(sides[0], ORB * s)
                    odd = pltpu.roll(sides[1], (ORB - ORB * s) % 128, 1)
                    B2[s, kind] = jnp.where(lane < ORB, even, odd)
                    B2[s + 4, kind] = lanes_from(own, NX * s)

        copies = []
        for d in range(1, SLABS):
            s = (slab + d) % SLABS
            copies.append(
                send(B2.at[s], R2.at[d - 1], r2_s.at[d - 1], r2_r.at[d - 1], to_slab(s))
            )
        return copies

    def finish(arrived):
        for copy in arrived:
            copy.wait_recv()
        for kind, out in enumerate((corr_ref, proj_ref)):
            block = B2[slab, kind]
            for d in range(SLABS - 1):
                block = block + R2[d, kind]
            out[...] = block[:, :NX] * (1.0 / CELLS)

    G[...] = jnp.zeros(G.shape, jnp.float32)
    stage_s(2)
    stage_s(6)
    stage_f(4)

    pl.semaphore_wait(barrier, len(partners))
    pots = [
        send(pot_ref.at[pl.ds(4, 8)], V_in.at[0], pot_s.at[0], pot_r.at[0], to_slab(up)),
        send(pot_ref.at[pl.ds(0, 8)], V_in.at[1], pot_s.at[1], pot_r.at[1], to_slab(down)),
    ]
    halos = []
    for t in range(3):
        halos.append((
            send(O.at[pl.ds(16 - 2 * t, 2)], O.at[pl.ds(4 - 2 * t, 2)],
                 halo_s.at[0, t], halo_r.at[0, t], to_slab(up)),
            send(O.at[pl.ds(6 + 2 * t, 2)], O.at[pl.ds(18 + 2 * t, 2)],
                 halo_s.at[1, t], halo_r.at[1, t], to_slab(down)),
        ))
    f0 = swap(0, 0)

    for copy in halos[0]:
        copy.wait_recv()
    stage_s(0, 10)
    stage_f(2, 8)
    f1 = swap(0, 1)
    stage_a(4)
    a0 = swap(1, 0)
    pass_on(0, f0)

    for copy in pots:
        copy.wait_recv()
    for n in range(4):
        fill(n - 4, V_in[0, 4 + n : 5 + n, :])
        fill(12 + n, V_in[1, n : n + 1, :])
    for copy in halos[1]:
        copy.wait_recv()
    stage_s(-2, 12)
    stage_f(0, 10)
    f2 = swap(0, 2)
    store = pltpu.make_async_copy(F.at[pl.ds(2, PLANES)], filt_hbm, out_sem)
    store.start()
    stage_a(2, 8)
    a1 = swap(1, 1)
    pass_on(1, f1)
    pass_on(3, a0)

    for copy in halos[2]:
        copy.wait_recv()
    stage_s(-4, 14)
    stage_f(-2, 12)
    stage_a(0, 10)
    a2 = swap(1, 2)
    pass_on(2, f2)

    forward(0, 0).wait_recv()
    gram_own(0)
    pass_far(1)

    @pl.when(jnp.logical_not(first))
    def _():
        wait_across(0)
        wait_across(3)
        gram(0, 1, 0, 1, RA_far)
        early().start()

    forward(1, 0).wait_recv()
    swap_wait(a1)
    gram_own(1)
    gram_far(1)
    pass_far(2)

    @pl.when(first)
    def _():
        early().wait_recv()
        G[1] = G[1] + G_far[...]

    forward(2, 0).wait_recv()
    swap_wait(a2)
    gram_own(2)
    gram_far(2)
    finish(reduce_slab(reduce_band()))

    for copy in sends:
        copy.wait_send()
    for q in range(3):
        forward(q, 0).wait_send()

    @pl.when(first)
    def _():
        for q in (1, 2):
            forward(q, 1).wait_send()
        for row in range(4):
            for side in range(2):
                cross(row, side).wait_send()
            across(0, row, landed(0, row)).wait_send()
            across(3, row, landed(3, row)).wait_send()

    @pl.when(jnp.logical_not(first))
    def _():
        for slot in (1, 2):
            for row in range(4):
                across(slot, row, landed(slot, row)).wait_send()
        early().wait_send()

    store.wait()


def local(orbitals, potential):
    f32 = jnp.float32
    dma = pltpu.SemaphoreType.DMA
    peers = len(PEERS)
    filtered, correlation, projected = pl.pallas_call(
        kernel,
        out_shape=(
            jax.ShapeDtypeStruct((PLANES, ORB, NXY), f32),
            jax.ShapeDtypeStruct((ORB, NX), f32),
            jax.ShapeDtypeStruct((ORB, NX), f32),
        ),
        in_specs=[
            pl.BlockSpec(memory_space=pl.ANY),
            pl.BlockSpec(memory_space=pltpu.VMEM),
            pl.BlockSpec(memory_space=pl.ANY),
        ],
        out_specs=(
            pl.BlockSpec(memory_space=pl.ANY),
            pl.BlockSpec(memory_space=pltpu.VMEM),
            pl.BlockSpec(memory_space=pltpu.VMEM),
        ),
        scratch_shapes=[
            pltpu.VMEM((PLANES + 12, ORB, NXY), f32),
            pltpu.VMEM((3, 512, 256), jnp.bfloat16),
            pltpu.VMEM((2, 8, NXY), f32),
            pltpu.VMEM((PLANES + 8, 8, NXY), f32),
            pltpu.VMEM((PLANES + 8, ORB, NXY), f32),
            pltpu.VMEM((PLANES + 4, ORB, NXY), f32),
            pltpu.VMEM((PLANES, ORB, NXY), f32),
            pltpu.VMEM((3, 2, 4, 2, ORB, NXY), f32),
            pltpu.VMEM((3, 4, ORB, NXY), f32),
            pltpu.VMEM((4, ORB, NXY), f32),
            pltpu.VMEM((2, 2, ROWS, HALF_ORB), f32),
            pltpu.VMEM((2, ROWS, HALF_ORB), f32),
            pltpu.VMEM((peers, 2, 2, ORB, HALF_ORB), f32),
            pltpu.VMEM((8, 2, ORB, 128), f32),
            pltpu.VMEM((8, 2, ORB, 128), f32),
            pltpu.VMEM((SLABS, 2, ORB, 128), f32),
            pltpu.VMEM((SLABS - 1, 2, ORB, 128), f32),
            dma, dma, dma,
            dma((2, 3)), dma((2, 3)),
            dma((2,)), dma((2,)),
            dma((2, 3, peers, 2)), dma((2, 3, peers, 2)),
            dma((2, 3, 2)),
            dma((3, 2)), dma((3, 2)),
            dma((4, 4)), dma((4, 4)),
            dma, dma,
            dma((peers,)), dma((peers,)),
            dma((8,)), dma((8,)),
            dma((SLABS - 1,)), dma((SLABS - 1,)),
        ],
        compiler_params=pltpu.CompilerParams(
            collective_id=0, has_side_effects=True, vmem_limit_bytes=56 << 20
        ),
        cost_estimate=pl.CostEstimate(
            flops=3_500_000_000, bytes_accessed=6_000_000, transcendentals=0
        ),
    )(jnp.transpose(orbitals, (1, 0, 2)), potential, plane_table())
    return jnp.transpose(filtered, (1, 0, 2)), correlation, projected


def solution(mesh):
    return jax.shard_map(
        local,
        mesh=mesh,
        in_specs=(P("band", "slab", None), P("slab", None)),
        out_specs=(P("band", "slab", None), P("band", "slab"), P("band", "slab")),
        check_vma=False,
    )
```

time: 442 us -> 112 us (0.25); the launches traced: 436 us -> 112 us
  waiting for transfers between devices: 240 us -> 0 us
  Pallas kernels: 0 us -> 107 us
  matrix products: 78.3 us -> 0 us
  local copies, waits for them, and re-layouts: 44 us -> 4.64 us
  other arithmetic: 36.2 us -> 0 us
  starting transfers between devices: 23.5 us -> 0 us
  between operations: 14.3 us -> 0.66 us
    all_gather x1 -> x0, waiting for transfers between devices: 196 us -> none  [local(): panel_piece = lax.all_gather(flat_filtered, 'band', axis=0, tiled=True)]
    pallas_call x0 -> x1, Pallas kernels: none -> 107 us  [local(): pl.pallas_call(kernel, out_shape=(jax.ShapeDtypeStruct((PLANES, ORB, NXY)...]
    dot_general x2 -> x0, matrix products: 78.3 us -> none  [the longest x1 39.1 us: local(): lax.dot_general(flat_applied, panel_piece, contract_dims, precision=lax.P...]
    unnamed x5 -> x0, waiting for transfers between devices: 33.2 us -> none
    slice x39 -> x0, local copies, waits for them, and re-layouts: 32.8 us -> none  [the longest x12 12.1 us: in_plane(): jnp.roll(grid_field, -offset, axis=-1)]
    ppermute x6 -> x0, starting transfers between devices: 23.4 us -> none  [the longest x3 21.6 us: extended_2(): lax.ppermute(lax.slice_in_dim(block, 0, width, axis=dim), axis, backward)]
    unnamed x1 -> x0, other arithmetic: 15.9 us -> none
    div x1 -> x0, other arithmetic: 10.4 us -> none  [local(): (apply_ham(extended(orbitals), potential, column_x) - CENTER * orbitals)...]
  transfers between devices with their start and end apart: 9 -> 0, of which waited for: 4 -> 0; matrix products, arithmetic and copies ran while one was open for 19% -> 0% of each run, Pallas kernels for 0% -> 0%
where the time goes in v2:
time: 112 us
  Pallas kernels  107 us (96%)
  local copies, waits for them, and re-layouts  4.64 us (4%)
    pallas_call x1, Pallas kernels, local(): pl.pallas_call(kernel, out_shape=(jax.ShapeDtypeStruct((PLANES, ORB, NXY)...  107 us
    unnamed x7, local copies, waits for them, and re-layouts  4.64 us

profile of v2, /device:TPU:0, one launch (start us, length us, event | category | flops | bytes accessed | tf_op | source)
XLA Modules:
  0.0 112.2 jit_solution(8943710789528498147)
XLA Ops:
  0.6 106.9 %shard_map.58 = (f32[12,24,2304]{2,1,0:T(8,128)}, f32[24,48]{1,0:T(8,128)}, f32[24,48]{1,0:T(8,128)}) custom-call(f32[12,24,2304]{2,1,0:T(8,128)} %bitcast.3, f32[12,2304]{1,0:T(8,128)} %pot_ref.1, bf16[3,512,256]{2,1,0:T(8,128)(2,1)} %constant.2.clone.table_hbm), custom_call_target="tpu_custom_call" | custom-call | flops 3500000000 | bytes 6000000 | tf_op jit(solution)/shard_map/pallas_call | solution.py:491
  107.5 0.0 copy-start.1
  107.5 0.0 copy-start
  107.5 3.4 %copy.9 = f32[24,12,2304]{2,0,1:T(8,128)} copy(f32[24,12,2304]{2,0,1:T(8,128)} %bitcast.2) | data formatting | bytes 5308416
  111.0 0.0 copy-done.1
  111.0 0.6 copy.10
  111.6 0.0 copy-done
  111.6 0.6 copy.11
Async XLA Ops:
  107.5 3.5 %copy-start.1 = (f32[24,48]{1,0:T(8,128)S(1)}, f32[24,48]{1,0:T(8,128)}, u32[]{:S(2)}) copy-start(f32[24,48]{1,0:T(8,128)} %get-tuple-element.13) | copy-start | bytes 13828
  107.5 4.0 %copy-start = (f32[24,48]{1,0:T(8,128)S(1)}, f32[24,48]{1,0:T(8,128)}, u32[]{:S(2)}) copy-start(f32[24,48]{1,0:T(8,128)} %get-tuple-element.14) | copy-start | bytes 13828

commit v3 on v2

--- a/solution.py
+++ b/solution.py
@@ -25,6 +25,8 @@
 
 CHUNK_BASE = (4, 2, 0)
 CHUNK_STRIDE = (0, 4, 8)
+ENDS = (3, 0)
+RELAYS = (1, 2)
 PEERS = (1, 3, 2)
 HALF_ORB = 192
 ROWS = 96
@@ -53,8 +55,8 @@
 
 def kernel(
     orb_hbm, pot_ref, table_hbm, filt_hbm, corr_ref, proj_ref,
-    O, T, V_in, W, S, F, A, RF, RA, RA_far, G, G_far, R1, XB, XR, B2, R2,
-    load_sem, table_sem, out_sem, halo_s, halo_r, pot_s, pot_r, swap_s, swap_r, own_sem, fwd_s, fwd_r,
+    O, relay, T, V_in, W, S, F, A, RF, RA, RA_far, G, G_far, SB, R1, XB, XR, B2, R2,
+    load_sem, table_sem, out_sem, halo_s, halo_r, relay_s, relay_r, pot_s, pot_r, swap_s, swap_r, own_sem, fwd_s, fwd_r,
     far_s, far_r, early_s, early_r, r1_s, r1_r, x_s, x_r, r2_s, r2_r,
 ):
     band, slab = lax.axis_index("band"), lax.axis_index("slab")
@@ -77,6 +79,37 @@
     partners.append(to_band(z_hi, y, 1 - core))
     partners += [to_band(1 - z_hi, row, side) for row in range(4) for side in range(2)]
     partners += [to_slab((slab + d) % SLABS) for d in range(1, SLABS)]
+    x_pos, z_lo = slab % 4, slab // 4
+
+    def halo_copy(src, dst, s_sem, r_sem, where):
+        return pltpu.make_async_remote_copy(
+            src_ref=src, dst_ref=dst, send_sem=s_sem, recv_sem=r_sem,
+            device_id=to_slab(where), device_id_type=MESH,
+        )
+
+    def outer(side):
+        return O.at[pl.ds((12, 10)[side], 2)], O.at[pl.ds((0, 22)[side], 2)]
+
+    def direct(side):
+        src, dst = outer(side)
+        return halo_copy(src, dst, halo_s.at[side, 2], halo_r.at[side, 2], (up, down)[side])
+
+    def to_relay(side):
+        return halo_copy(outer(side)[0], relay.at[side], halo_s.at[side, 2], relay_r.at[side],
+                         (1 - z_lo) * 4 + RELAYS[side])
+
+    def from_relay(side):
+        return halo_copy(relay.at[side], outer(side)[1], relay_s.at[side], halo_r.at[side, 2],
+                         z_lo * 4 + ENDS[1 - side])
+
+    def pass_halo():
+        for side in range(2):
+
+            @pl.when(x_pos == RELAYS[side])
+            def _():
+                to_relay(side).wait_recv()
+                from_relay(side).start()
+
     barrier = pltpu.get_barrier_semaphore()
     for partner in partners:
         pl.semaphore_signal(barrier, inc=1, device_id=partner, device_id_type=MESH)
@@ -251,27 +284,32 @@
             wait_across(q)
             forward(q, 1).start()
 
-    def gram(q, half, columns, f_rows, a_rows):
+    def gram(q, half, columns, f_rows, a_rows, kinds=(0, 1)):
+        count = len(kinds) * ROWS
+
         def body(k, carry):
             lanes = pl.ds(pl.multiple_of(k * CHUNK, 128), CHUNK)
             f_high, f_low = halves(RF[q, columns, :, :, :, lanes].reshape(HALF_ORB, CHUNK))
-            rows = jnp.concatenate([RF[q, f_rows, :, core, :, lanes], a_rows[:, :, lanes]], axis=0)
-            high, low = halves(rows.reshape(2 * ROWS, CHUNK))
+            rows = [RF[q, f_rows, :, core, :, lanes] if kind == 0 else a_rows[:, :, lanes] for kind in kinds]
+            rows = rows[0] if len(kinds) == 1 else jnp.concatenate(rows, axis=0)
+            high, low = halves(rows.reshape(count, CHUNK))
             both = dot_nt(jnp.concatenate([high, low], axis=0), f_high)
-            part = (both[: 2 * ROWS] + both[2 * ROWS :]) + dot_nt(high, f_low)
-            G[half] = G[half] + part.reshape(2, ROWS, HALF_ORB)
+            part = (both[:count] + both[count:]) + dot_nt(high, f_low)
+            for n, kind in enumerate(kinds):
+                G[half, kind] = G[half, kind] + part[n * ROWS : (n + 1) * ROWS]
             return carry
 
         lax.fori_loop(0, NXY // CHUNK, body, 0)
 
-    def gram_own(q):
-        gram(q, 0, 0, 0, RA.at[q])
-
-    def gram_far(q):
+    def gram_own(q, kinds=(0, 1)):
+        gram(q, 0, 0, 0, RA.at[q], kinds)
+
+    def gram_far(q, kinds=(0, 1), wait=True):
         @pl.when(first)
         def _():
-            forward(q, 1).wait_recv()
-            gram(q, 1, 1, 0, RA.at[q])
+            if wait:
+                forward(q, 1).wait_recv()
+            gram(q, 1, 1, 0, RA.at[q], kinds)
 
     def early():
         return pltpu.make_async_remote_copy(
@@ -279,87 +317,86 @@
             device_id=to_band(1 - z_hi, y, core), device_id_type=MESH,
         )
 
-    def panel(row):
-        return G.at[:, :, pl.ds(pl.multiple_of(row * ORB, 8), ORB)]
-
-    def cross(row, side):
+    def to_row(kind, d, width):
+        row = (y + d) % 4
+        return pltpu.make_async_remote_copy(
+            src_ref=SB.at[kind, pl.ds(pl.multiple_of(row * ORB, 8), ORB), pl.ds(0, width)],
+            dst_ref=R1.at[kind, d - 1, :, pl.ds(0, width)],
+            send_sem=r1_s.at[kind, d - 1], recv_sem=r1_r.at[kind, d - 1],
+            device_id=to_band(z_hi, row, core), device_id_type=MESH,
+        )
+
+    def cross(kind, row, side):
         index = row * 2 + side
         return pltpu.make_async_remote_copy(
-            src_ref=XB.at[index], dst_ref=XR.at[y * 2 + core],
-            send_sem=x_s.at[index], recv_sem=x_r.at[y * 2 + core],
+            src_ref=XB.at[kind, index], dst_ref=XR.at[kind, y * 2 + core],
+            send_sem=x_s.at[kind, index], recv_sem=x_r.at[kind, y * 2 + core],
             device_id=to_band(1 - z_hi, row, side), device_id_type=MESH,
         )
 
-    def cross_from(index):
+    def cross_from(kind, index):
         return pltpu.make_async_remote_copy(
-            src_ref=XB.at[index], dst_ref=XR.at[index],
-            send_sem=x_s.at[index], recv_sem=x_r.at[index],
+            src_ref=XB.at[kind, index], dst_ref=XR.at[kind, index],
+            send_sem=x_s.at[kind, index], recv_sem=x_r.at[kind, index],
             device_id=to_band(1 - z_hi, index // 2, index % 2), device_id_type=MESH,
         )
 
-    def reduce_band():
-        copies = []
-        for d in PEERS:
-            row = (y + d) % 4
-            copies.append(
-                send(panel(row), R1.at[d - 1], r1_s.at[d - 1], r1_r.at[d - 1], to_band(z_hi, row, core))
-            )
+    def reduce_band(kind):
+        SB[kind] = jnp.concatenate([G[0, kind], G[1, kind]], axis=1)
 
         @pl.when(first)
         def _():
-            for kind in range(2):
-                block = jnp.concatenate(
-                    [G[1, kind], jnp.zeros((128 - ROWS, HALF_ORB), jnp.float32)], axis=0
-                )
-                XB[:, kind] = jnp.transpose(block).reshape(8, ORB, 128)
+            for d in PEERS:
+                to_row(kind, d, 384).start()
+            block = jnp.concatenate([G[1, kind], jnp.zeros((128 - ROWS, HALF_ORB), jnp.float32)], axis=0)
+            XB[kind] = jnp.transpose(block).reshape(8, ORB, 128)
             for row in range(4):
                 for side in range(2):
-                    cross(row, side).start()
-
-        return copies
+                    cross(kind, row, side).start()
+
+        @pl.when(jnp.logical_not(first))
+        def _():
+            for d in PEERS:
+                to_row(kind, d, 256).start()
 
     lane = lax.broadcasted_iota(jnp.int32, (ORB, 128), 1)
 
     def lanes_from(value, start):
         return pltpu.roll(value, (-start) % value.shape[1], 1)[:, :128]
 
-    def reduce_slab(arrived):
-        for copy in arrived:
-            copy.wait_recv()
+    def reduce_rows(kind):
         mine = pl.ds(pl.multiple_of(y * ORB, 8), ORB)
 
-        def rows_of(half, kind):
-            rows = G[half, kind, mine]
-            for d in range(len(PEERS)):
-                rows = rows + R1[d, half, kind]
-            return jnp.concatenate([rows, jnp.zeros((ORB, 64), jnp.float32)], axis=1)
-
         @pl.when(first)
         def _():
-            for kind in range(2):
-                own, other = rows_of(0, kind), rows_of(1, kind)
-                for s in range(4):
-                    B2[s, kind] = lanes_from(own, NX * s)
-                    B2[s + 4, kind] = lanes_from(other, NX * s)
+            rows = SB[kind, mine]
+            for d in PEERS:
+                to_row(kind, d, 384).wait_recv()
+                rows = rows + R1[kind, d - 1]
+            for s in range(SLABS):
+                B2[s, kind] = lanes_from(rows, NX * s)
 
         @pl.when(jnp.logical_not(first))
         def _():
+            rows = SB[kind, mine, pl.ds(0, 256)]
+            for d in PEERS:
+                to_row(kind, d, 256).wait_recv()
+                rows = rows + R1[kind, d - 1, :, pl.ds(0, 256)]
             for index in range(8):
-                cross_from(index).wait_recv()
-            for kind in range(2):
-                own = rows_of(0, kind)
-                sides = []
-                for side in range(2):
-                    total = XR[side, kind]
-                    for row in range(1, 4):
-                        total = total + XR[2 * row + side, kind]
-                    sides.append(total)
-                for s in range(4):
-                    even = lanes_from(sides[0], ORB * s)
-                    odd = pltpu.roll(sides[1], (ORB - ORB * s) % 128, 1)
-                    B2[s, kind] = jnp.where(lane < ORB, even, odd)
-                    B2[s + 4, kind] = lanes_from(own, NX * s)
-
+                cross_from(kind, index).wait_recv()
+            sides = []
+            for side in range(2):
+                total = XR[kind, side]
+                for row in range(1, 4):
+                    total = total + XR[kind, 2 * row + side]
+                sides.append(total)
+            for s in range(4):
+                even = lanes_from(sides[0], ORB * s)
+                odd = pltpu.roll(sides[1], (ORB - ORB * s) % 128, 1)
+                B2[s, kind] = jnp.where(lane < ORB, even, odd)
+                B2[s + 4, kind] = lanes_from(rows, NX * s)
+
+    def reduce_slab():
         copies = []
         for d in range(1, SLABS):
             s = (slab + d) % SLABS
@@ -388,13 +425,23 @@
         send(pot_ref.at[pl.ds(0, 8)], V_in.at[1], pot_s.at[1], pot_r.at[1], to_slab(down)),
     ]
     halos = []
-    for t in range(3):
+    for t in range(2):
         halos.append((
             send(O.at[pl.ds(16 - 2 * t, 2)], O.at[pl.ds(4 - 2 * t, 2)],
                  halo_s.at[0, t], halo_r.at[0, t], to_slab(up)),
             send(O.at[pl.ds(6 + 2 * t, 2)], O.at[pl.ds(18 + 2 * t, 2)],
                  halo_s.at[1, t], halo_r.at[1, t], to_slab(down)),
         ))
+    for side in range(2):
+
+        @pl.when(x_pos == ENDS[side])
+        def _():
+            to_relay(side).start()
+
+        @pl.when(x_pos != ENDS[side])
+        def _():
+            direct(side).start()
+
     f0 = swap(0, 0)
 
     for copy in halos[0]:
@@ -421,14 +468,15 @@
     stage_a(2, 8)
     a1 = swap(1, 1)
     pass_on(1, f1)
-    pass_on(3, a0)
-
-    for copy in halos[2]:
-        copy.wait_recv()
+    pass_halo()
+
+    for side in range(2):
+        direct(side).wait_recv()
     stage_s(-4, 14)
     stage_f(-2, 12)
     stage_a(0, 10)
     a2 = swap(1, 2)
+    pass_on(3, a0)
     pass_on(2, f2)
 
     forward(0, 0).wait_recv()
@@ -446,6 +494,8 @@
     swap_wait(a1)
     gram_own(1)
     gram_far(1)
+    forward(2, 0).wait_recv()
+    gram_own(2, (0,))
     pass_far(2)
 
     @pl.when(first)
@@ -453,14 +503,25 @@
         early().wait_recv()
         G[1] = G[1] + G_far[...]
 
-    forward(2, 0).wait_recv()
+    gram_far(2, (0,))
+    reduce_band(0)
     swap_wait(a2)
-    gram_own(2)
-    gram_far(2)
-    finish(reduce_slab(reduce_band()))
+    gram_own(2, (1,))
+    gram_far(2, (1,), False)
+    reduce_band(1)
+    reduce_rows(0)
+    reduce_rows(1)
+    finish(reduce_slab())
 
     for copy in sends:
         copy.wait_send()
+    for side in range(2):
+        direct(side).wait_send()
+
+        @pl.when(x_pos == RELAYS[side])
+        def _():
+            from_relay(side).wait_send()
+
     for q in range(3):
         forward(q, 0).wait_send()
 
@@ -468,9 +529,13 @@
     def _():
         for q in (1, 2):
             forward(q, 1).wait_send()
+        for kind in range(2):
+            for d in PEERS:
+                to_row(kind, d, 384).wait_send()
+            for row in range(4):
+                for side in range(2):
+                    cross(kind, row, side).wait_send()
         for row in range(4):
-            for side in range(2):
-                cross(row, side).wait_send()
             across(0, row, landed(0, row)).wait_send()
             across(3, row, landed(3, row)).wait_send()
 
@@ -480,6 +545,9 @@
             for row in range(4):
                 across(slot, row, landed(slot, row)).wait_send()
         early().wait_send()
+        for kind in range(2):
+            for d in PEERS:
+                to_row(kind, d, 256).wait_send()
 
     store.wait()
 
@@ -488,25 +556,27 @@
     f32 = jnp.float32
     dma = pltpu.SemaphoreType.DMA
     peers = len(PEERS)
-    filtered, correlation, projected = pl.pallas_call(
+    shapes = (
+        pltpu.VMEM((PLANES, ORB, NXY), f32),
+        pltpu.VMEM((ORB, NX), f32),
+        pltpu.VMEM((ORB, NX), f32),
+    )
+    results = pl.pallas_call(
         kernel,
-        out_shape=(
-            jax.ShapeDtypeStruct((PLANES, ORB, NXY), f32),
-            jax.ShapeDtypeStruct((ORB, NX), f32),
-            jax.ShapeDtypeStruct((ORB, NX), f32),
-        ),
+        out_shape=shapes,
         in_specs=[
             pl.BlockSpec(memory_space=pl.ANY),
             pl.BlockSpec(memory_space=pltpu.VMEM),
             pl.BlockSpec(memory_space=pl.ANY),
         ],
         out_specs=(
-            pl.BlockSpec(memory_space=pl.ANY),
+            pl.BlockSpec(memory_space=pltpu.VMEM),
             pl.BlockSpec(memory_space=pltpu.VMEM),
             pl.BlockSpec(memory_space=pltpu.VMEM),
         ),
         scratch_shapes=[
             pltpu.VMEM((PLANES + 12, ORB, NXY), f32),
+            pltpu.VMEM((2, 2, ORB, NXY), f32),
             pltpu.VMEM((3, 512, 256), jnp.bfloat16),
             pltpu.VMEM((2, 8, NXY), f32),
             pltpu.VMEM((PLANES + 8, 8, NXY), f32),
@@ -518,21 +588,23 @@
             pltpu.VMEM((4, ORB, NXY), f32),
             pltpu.VMEM((2, 2, ROWS, HALF_ORB), f32),
             pltpu.VMEM((2, ROWS, HALF_ORB), f32),
-            pltpu.VMEM((peers, 2, 2, ORB, HALF_ORB), f32),
-            pltpu.VMEM((8, 2, ORB, 128), f32),
-            pltpu.VMEM((8, 2, ORB, 128), f32),
+            pltpu.VMEM((2, ROWS, 2 * HALF_ORB), f32),
+            pltpu.VMEM((2, peers, ORB, 2 * HALF_ORB), f32),
+            pltpu.VMEM((2, 8, ORB, 128), f32),
+            pltpu.VMEM((2, 8, ORB, 128), f32),
             pltpu.VMEM((SLABS, 2, ORB, 128), f32),
             pltpu.VMEM((SLABS - 1, 2, ORB, 128), f32),
             dma, dma, dma,
             dma((2, 3)), dma((2, 3)),
+            dma((2,)), dma((2,)),
             dma((2,)), dma((2,)),
             dma((2, 3, peers, 2)), dma((2, 3, peers, 2)),
             dma((2, 3, 2)),
             dma((3, 2)), dma((3, 2)),
             dma((4, 4)), dma((4, 4)),
             dma, dma,
-            dma((peers,)), dma((peers,)),
-            dma((8,)), dma((8,)),
+            dma((2, peers)), dma((2, peers)),
+            dma((2, 8)), dma((2, 8)),
             dma((SLABS - 1,)), dma((SLABS - 1,)),
         ],
         compiler_params=pltpu.CompilerParams(
@@ -542,6 +614,7 @@
             flops=3_500_000_000, bytes_accessed=6_000_000, transcendentals=0
         ),
     )(jnp.transpose(orbitals, (1, 0, 2)), potential, plane_table())
+    filtered, correlation, projected = results
     return jnp.transpose(filtered, (1, 0, 2)), correlation, projected
 
 

time: 112 us -> 106 us (0.946)
  Pallas kernels: 107 us -> 103 us
  local copies, waits for them, and re-layouts: 4.64 us -> 2.7 us
    pallas_call x1, Pallas kernels: 107 us -> 103 us  [local(): pl.pallas_call(kernel, out_shape=shapes, in_specs=[pl.BlockSpec(memory_sp...]
    unnamed x7 -> x3, local copies, waits for them, and re-layouts: 4.64 us -> 2.7 us
where the time goes in v3:
time: 106 us
  Pallas kernels  103 us (97%)
  local copies, waits for them, and re-layouts  2.7 us (3%)
    pallas_call x1, Pallas kernels, local(): pl.pallas_call(kernel, out_shape=shapes, in_specs=[pl.BlockSpec(memory_sp...  103 us
    unnamed x3, local copies, waits for them, and re-layouts  2.7 us

profile of v3, /device:TPU:0, one launch (start us, length us, event | category | flops | bytes accessed | tf_op | source)
XLA Modules:
  0.0 105.9 jit_solution(3277350790049447634)
XLA Ops:
  0.6 102.6 %shard_map.58 = (f32[12,24,2304]{2,1,0:T(8,128)S(1)}, f32[24,48]{1,0:T(8,128)S(1)}, f32[24,48]{1,0:T(8,128)S(1)}) custom-call(f32[12,24,2304]{2,1,0:T(8,128)} %bitcast.3, f32[12,2304]{1,0:T(8,128)} %pot_ref.1, bf16[3,512,256]{2,1,0:T(8,128)(2,1)} %constant.2.clone.table_hbm), custom_call_target="tpu_custom_call" | custom-call | flops 3500000000 | bytes 6000000 | tf_op jit(solution)/shard_map/pallas_call | solution.py:564
  103.2 1.5 %copy.9 = f32[24,12,2304]{2,0,1:T(8,128)} copy(f32[24,12,2304]{2,0,1:T(8,128)S(1)} %bitcast.2) | data formatting | bytes 5308416
  104.7 0.6 copy.10
  105.3 0.6 copy.11

commit v4 on v3

--- a/solution.py
+++ b/solution.py
@@ -288,18 +288,18 @@
         count = len(kinds) * ROWS
 
         def body(k, carry):
-            lanes = pl.ds(pl.multiple_of(k * CHUNK, 128), CHUNK)
-            f_high, f_low = halves(RF[q, columns, :, :, :, lanes].reshape(HALF_ORB, CHUNK))
+            lanes = pl.ds(pl.multiple_of(k * 1152, 128), 1152)
+            f_high, f_low = halves(RF[q, columns, :, :, :, lanes].reshape(HALF_ORB, 1152))
             rows = [RF[q, f_rows, :, core, :, lanes] if kind == 0 else a_rows[:, :, lanes] for kind in kinds]
             rows = rows[0] if len(kinds) == 1 else jnp.concatenate(rows, axis=0)
-            high, low = halves(rows.reshape(count, CHUNK))
+            high, low = halves(rows.reshape(count, 1152))
             both = dot_nt(jnp.concatenate([high, low], axis=0), f_high)
             part = (both[:count] + both[count:]) + dot_nt(high, f_low)
             for n, kind in enumerate(kinds):
                 G[half, kind] = G[half, kind] + part[n * ROWS : (n + 1) * ROWS]
             return carry
 
-        lax.fori_loop(0, NXY // CHUNK, body, 0)
+        lax.fori_loop(0, NXY // 1152, body, 0)
 
     def gram_own(q, kinds=(0, 1)):
         gram(q, 0, 0, 0, RA.at[q], kinds)

time: 106 us -> 103 us (0.972)
  Pallas kernels: 103 us -> 99.8 us
    pallas_call x1, Pallas kernels: 103 us -> 99.8 us  [local(): pl.pallas_call(kernel, out_shape=shapes, in_specs=[pl.BlockSpec(memory_sp...]
where the time goes in v4:
time: 103 us
  Pallas kernels  99.8 us (97%)
  local copies, waits for them, and re-layouts  2.7 us (3%)
    pallas_call x1, Pallas kernels, local(): pl.pallas_call(kernel, out_shape=shapes, in_specs=[pl.BlockSpec(memory_sp...  99.8 us
    unnamed x3, local copies, waits for them, and re-layouts  2.7 us

profile of v4, /device:TPU:0, one launch (start us, length us, event | category | flops | bytes accessed | tf_op | source)
XLA Modules:
  0.0 103.1 jit_solution(7726573844956312393)
XLA Ops:
  0.6 99.8 %shard_map.58 = (f32[12,24,2304]{2,1,0:T(8,128)S(1)}, f32[24,48]{1,0:T(8,128)S(1)}, f32[24,48]{1,0:T(8,128)S(1)}) custom-call(f32[12,24,2304]{2,1,0:T(8,128)} %bitcast.3, f32[12,2304]{1,0:T(8,128)} %pot_ref.1, bf16[3,512,256]{2,1,0:T(8,128)(2,1)} %constant.2.clone.table_hbm), custom_call_target="tpu_custom_call" | custom-call | flops 3500000000 | bytes 6000000 | tf_op jit(solution)/shard_map/pallas_call | solution.py:564
  100.4 1.5 %copy.9 = f32[24,12,2304]{2,0,1:T(8,128)} copy(f32[24,12,2304]{2,0,1:T(8,128)S(1)} %bitcast.2) | data formatting | bytes 5308416
  101.9 0.6 copy.10
  102.5 0.6 copy.11

commit v5 on v4

--- a/solution.py
+++ b/solution.py
@@ -476,8 +476,8 @@
     stage_f(-2, 12)
     stage_a(0, 10)
     a2 = swap(1, 2)
+    pass_on(2, f2)
     pass_on(3, a0)
-    pass_on(2, f2)
 
     forward(0, 0).wait_recv()
     gram_own(0)

time: 103 us -> 103 us (level)
  no operation moved by 1% of the time
where the time goes in v5:
time: 103 us
  Pallas kernels  99.9 us (97%)
  local copies, waits for them, and re-layouts  2.7 us (3%)
    pallas_call x1, Pallas kernels, local(): pl.pallas_call(kernel, out_shape=shapes, in_specs=[pl.BlockSpec(memory_sp...  99.9 us
    unnamed x3, local copies, waits for them, and re-layouts  2.7 us

profile of v5, /device:TPU:0, one launch (start us, length us, event | category | flops | bytes accessed | tf_op | source)
XLA Modules:
  0.0 103.3 jit_solution(5939784487451144230)
XLA Ops:
  0.6 99.9 %shard_map.58 = (f32[12,24,2304]{2,1,0:T(8,128)S(1)}, f32[24,48]{1,0:T(8,128)S(1)}, f32[24,48]{1,0:T(8,128)S(1)}) custom-call(f32[12,24,2304]{2,1,0:T(8,128)} %bitcast.3, f32[12,2304]{1,0:T(8,128)} %pot_ref.1, bf16[3,512,256]{2,1,0:T(8,128)(2,1)} %constant.2.clone.table_hbm), custom_call_target="tpu_custom_call" | custom-call | flops 3500000000 | bytes 6000000 | tf_op jit(solution)/shard_map/pallas_call | solution.py:564
  100.6 1.5 %copy.9 = f32[24,12,2304]{2,0,1:T(8,128)} copy(f32[24,12,2304]{2,0,1:T(8,128)S(1)} %bitcast.2) | data formatting | bytes 5308416
  102.1 0.6 copy.10
  102.7 0.6 copy.11
